TPU v7x, 512 devices: a whole 4x4x16 slice. The times are simulated.
512 devices in a mesh: row: 16 (over y, z_hi, core), col: 32 (over x, z_lo).
Axes of the slice: x: 4, y: 4, z: 16 (z_hi: 2, z_lo: 8; z = z_hi * 8 + z_lo), core: 2. Of those that a mesh axis runs over, the one named last changes fastest.
Arguments:
- amplitudes: bfloat16 [96, 16384], P(None, ('row', 'col')), may hold values from -6 to 6
- integrals: bfloat16 [16384, 16384], P('row', 'col'), may hold values from -0.046875 to 0.046875
- owner: int32 [128, 128], replicated, may hold values from 0 to 1, as said below
Outputs:
- residual: float32 [96, 16384], P(None, ('row', 'col'))
Inputs may be any that keep to these rules, and one draw needn't show every extreme that they name: owner[I, J] + owner[J, I] = 1 for I != J, and owner[I, I] = 1.
All inputs are finite; a program needn't handle non-finite values.
Results may differ from a plain program's by a relative error of at most 0.0003.
Values may be sent and summed in bfloat16 or wider, within the bound.
A program may use at most 64 MiB of HBM per device.

v0:
```python
import jax
import jax.numpy as jnp
from jax import lax
from jax.sharding import PartitionSpec as P

TB = 128


def local(amplitudes, integrals, owner):
    pair_rows, pair_cols = integrals.shape
    row_tiles = pair_rows // TB
    col_tiles = pair_cols // TB
    row_index = lax.axis_index("row")
    col_index = lax.axis_index("col")
    first_row = row_index * pair_rows
    first_col = col_index * pair_cols
    source_row = first_col // pair_rows
    offset = first_col - source_row * pair_rows
    everything = lax.all_gather(amplitudes, ("row", "col"), axis=1, tiled=True)
    row_amps = lax.dynamic_slice_in_dim(everything, first_row, pair_rows, 1)
    col_amps = lax.dynamic_slice_in_dim(everything, first_col, pair_cols, 1)
    local_owner = lax.dynamic_slice(
        owner, (row_index * row_tiles, col_index * col_tiles), (row_tiles, col_tiles)
    )
    block_rows = row_index * row_tiles + jnp.arange(row_tiles, dtype=jnp.int32)[:, None]
    block_cols = col_index * col_tiles + jnp.arange(col_tiles, dtype=jnp.int32)[None, :]
    tile_grid = integrals.reshape(row_tiles, TB, col_tiles, TB)
    zero_tiles = jnp.zeros_like(tile_grid)
    kept_tiles = jnp.where((local_owner == 1)[:, None, :, None], tile_grid, zero_tiles).reshape(
        pair_rows, pair_cols
    )
    away_mask = (local_owner == 1) & (block_rows != block_cols)
    away_tiles = jnp.where(away_mask[:, None, :, None], tile_grid, zero_tiles).reshape(
        pair_rows, pair_cols
    )
    row_terms = lax.dot_general(
        col_amps, kept_tiles, (((1,), (1,)), ((), ())), preferred_element_type=jnp.float32
    )
    col_terms = jnp.dot(row_amps, away_tiles, preferred_element_type=jnp.float32)
    col_total = lax.psum(col_terms, "row")
    placed = lax.dynamic_update_slice_in_dim(jnp.zeros_like(row_terms), col_total, offset, 1)
    placed = jnp.where(row_index == source_row, placed, jnp.zeros_like(placed))
    return lax.psum_scatter(row_terms + placed, "col", scatter_dimension=1, tiled=True)


def solution(mesh):
    in_specs = (P(None, ("row", "col")), P("row", "col"), P())
    out_specs = P(None, ("row", "col"))
    return jax.shard_map(local, mesh=mesh, in_specs=in_specs, out_specs=out_specs, check_vma=False)
```

profile of v0, /device:TPU:1, one launch (start us, length us, event | category | flops | bytes accessed | tf_op | source)
XLA Modules:
  0.0 1877.5 jit_solution(9118374515881627747)
XLA Ops:
  6.5 0.0 copy-start
  6.5 0.0 all-gather.2.cloned.1.call-start
  6.5 0.7 all-gather.2.cloned.1.call-update
  7.3 0.0 all-reduce.2.cloned.1.call-start
  7.4 0.8 compare_and_fusion
  8.1 1395.1 %all-gather.2.cloned.1.call-done = bf16[96,16384]{0,1:T(8,128)(2,1)} async-done(((bf16[96,32]{0,1:T(8,128)(2,1)}), bf16[96,16384]{0,1:T(8,128)(2,1)}) %all-gather.2.cloned.1.call-update) | async-done | bytes 3145744 | tf_op jit(solution)/shard_map/all_gather | solution.py:19
  1403.2 0.3 broadcast_in_dim.27
  1403.6 2.5 fusion.1
  1406.1 0.0 all-reduce.2.cloned.1.call-update
  1406.1 0.0 reduce-scatter.4.cloned.1.call-start
  1406.2 0.3 broadcast_in_dim.24
  1406.5 0.0 copy-done
  1406.5 1.4 fusion
  1407.9 245.9 %all-reduce.2.cloned.1.call-done = f32[96,512]{1,0:T(8,128)} async-done(((f32[96,512]{1,0:T(8,128)}), f32[96,512]{1,0:T(8,128)}) %all-reduce.2.cloned.1.call-update) | async-done | bytes 196624 | tf_op jit(solution)/shard_map/psum | solution.py:40
  1653.9 1.0 copy.6
  1654.9 0.0 reduce-scatter.4.cloned.1.call-update
  1654.9 216.1 %reduce-scatter.4.cloned.1.call-done = f32[32,96]{1,0:T(8,128)} async-done(((f32[1024,96]{1,0:T(8,128)}), f32[32,96]{1,0:T(8,128)}) %reduce-scatter.4.cloned.1.call-update) | async-done | bytes 12304
  (3 shorter events, 0.1 us)
Async XLA Ops:
  6.5 1400.0 %copy-start = (bf16[1024,512]{1,0:T(8,128)(2,1)S(1)}, bf16[1024,512]{1,0:T(8,128)(2,1)}, u32[]{:S(2)}) copy-start(bf16[1024,512]{1,0:T(8,128)(2,1)} %param.4) | copy-start | bytes 3145732
  6.5 1396.7 %all-gather.2.cloned.1.call-start = ((), (), s32[]{:S(2)}) async-start(), calls=%async_computation.1 | async-start | bytes 4202496 | tf_op jit(solution)/shard_map/all_gather | solution.py:19
  7.3 1646.6 %all-reduce.2.cloned.1.call-start = ((), (), s32[]{:S(2)}) async-start(), calls=%async_computation.2 | async-start | bytes 393216 | tf_op jit(solution)/shard_map/psum | solution.py:40
  1406.1 464.8 %reduce-scatter.4.cloned.1.call-start = ((), (), s32[]{:S(2)}) async-start(), calls=%async_computation.3 | async-start | bytes 540672
Sparse Core Ops, SparseCore 0:
  9.6 1393.6 all-gather.1
  1406.2 247.5 all-reduce.1
  1656.8 214.0 reduce-scatter.3
where the time goes:
time: 1900 us; the launch traced here: 1880 us
  waiting for transfers between devices  1860 us (98%)
    all_gather x1, waiting for transfers between devices, local(): everything = lax.all_gather(amplitudes, ('row', 'col'), axis=1, tiled=True)  1400 us
    psum x1, waiting for transfers between devices, local(): col_total = lax.psum(col_terms, 'row')  246 us
    unnamed x4, waiting for transfers between devices  217 us
  transfers between devices with their start and end apart: 3, of which 3 were waited for; matrix products, arithmetic and copies ran while one was open for 0% of the time, Pallas kernels for 0%

commit v1 on v0

v1 whole, which is shorter than its diff:
```python
import functools

import jax
import jax.numpy as jnp
from jax import lax
from jax.experimental import pallas as pl
from jax.experimental.pallas import tpu as pltpu
from jax.sharding import PartitionSpec as P

TB = 128
LANES = 128
XN, ZN = 4, 8
MESH = pl.DeviceIdType.MESH
F32 = jnp.float32
BF16 = jnp.bfloat16


def pack(block, occ):
    lane = lax.broadcasted_iota(jnp.int32, (8, LANES), 1)
    out = []
    for s in range(block.shape[0] // 32):
        last = block[s * 32 + 24 : s * 32 + 32]
        for j in range(3):
            moved = pltpu.roll(last, occ - 32 * j, 1)
            out.append(jnp.where(lane < occ, block[s * 32 + 8 * j : s * 32 + 8 * j + 8], moved))
    return jnp.concatenate(out, axis=0)


def unpack(block, occ):
    lane = lax.broadcasted_iota(jnp.int32, (8, LANES), 1)
    last = jnp.zeros((8, LANES), F32)
    for j in range(3):
        moved = pltpu.roll(block[8 * j : 8 * j + 8], (LANES - occ + 32 * j) % LANES, 1)
        last = jnp.where((lane >= 32 * j) & (lane < 32 * j + 32), moved, last)
    return jnp.concatenate([block, last], axis=0)


def kernel(
    amp_ref, w_hbm, owner_hbm, out_ref,
    w_v, wat, own_s, ar, ac, row_send, x_recv, col_half, sib_recv, cross_send, cross_recv, z_send, z_recv,
    w_sem, own_sem, sems_a, sems_b, sems_c, sems_d, sems_e,
):
    occ, shard = amp_ref.shape
    rows, cols = w_v.shape
    row_tiles, col_tiles = rows // TB, cols // TB
    chunk = rows // XN
    packed = chunk * 3 // 4
    piece = packed // ZN
    r = lax.axis_index("row")
    c = lax.axis_index("col")
    y, zh, core = r // 4, (r // 2) % 2, r % 2
    x, zl = c // 8, c % 8

    def at(yy, zz, cc, xx, ll):
        return (yy * 4 + zz * 2 + cc, xx * 8 + ll)

    z_peers = [at(y, zh, core, x, zl ^ k) for k in range(1, ZN)]
    x_peers = [at(y, zh, core, x ^ k, zl) for k in range(1, XN)]
    sibling = at(y, zh, 1 - core, x, zl)
    target = at((zl % 4) ^ 1, zl // 4, x % 2, y, 4 * zh + 2 * core + x // 2)
    source = at(x, zl // 4, (zl // 2) % 2, 2 * (zl % 2) + core, 4 * zh + (y ^ 1))

    w_copy = pltpu.make_async_copy(w_hbm, w_v, w_sem)
    w_copy.start()
    own_copy = pltpu.make_async_copy(owner_hbm.at[pl.ds(r * row_tiles, row_tiles)], own_s, own_sem)
    own_copy.start()

    eye = (
        lax.broadcasted_iota(jnp.int32, (shard, shard), 0) == lax.broadcasted_iota(jnp.int32, (shard, shard), 1)
    ).astype(F32).astype(BF16)
    wide = jnp.concatenate([amp_ref[...], jnp.zeros((LANES - occ, shard), BF16)], axis=0)
    turned = lax.dot_general(eye, wide, (((1,), (1,)), ((), ())), preferred_element_type=F32)
    mine = pl.ds(pl.multiple_of(x * chunk + zl * shard, shard), shard)
    ar[mine, :] = turned.astype(BF16)

    barrier = pltpu.get_barrier_semaphore()
    partners = z_peers + x_peers + [sibling, target, source]
    for peer in partners:
        pl.semaphore_signal(barrier, inc=1, device_id=peer, device_id_type=MESH)
    pl.semaphore_wait(barrier, len(partners))

    def send(src, dst, sems, k, peer):
        copy = pltpu.make_async_remote_copy(
            src_ref=src, dst_ref=dst, send_sem=sems.at[0, k], recv_sem=sems.at[1, k],
            device_id=peer, device_id_type=MESH,
        )
        copy.start()
        return copy

    za = [send(ar.at[mine], ar.at[mine], sems_a, k, z_peers[k]) for k in reversed(range(ZN - 1))]

    w_copy.wait()
    own_copy.wait()
    for i in range(row_tiles):
        for j in range(col_tiles):
            held = own_s[i, c * col_tiles + j] == 1
            tile = w_v[i * TB : (i + 1) * TB, j * TB : (j + 1) * TB]
            kept = jnp.where(held, tile, jnp.zeros_like(tile))
            w_v[i * TB : (i + 1) * TB, j * TB : (j + 1) * TB] = kept
            away = jnp.where(r * row_tiles + i == c * col_tiles + j, jnp.zeros_like(tile), kept)
            wat[j * TB : (j + 1) * TB, i * TB : (i + 1) * TB] = away.T
    for copy in za:
        copy.wait()

    own_chunk = pl.ds(pl.multiple_of(x * chunk, chunk), chunk)
    cross_in = send(
        ar.at[own_chunk], ac.at[pl.ds(pl.multiple_of((x % 2) * chunk, chunk), chunk)], sems_c, 0, target
    )
    xa = [send(ar.at[own_chunk], ar.at[own_chunk], sems_b, k, x_peers[k]) for k in (1, 0, 2)]

    cross_in.wait()
    half = pl.ds(pl.multiple_of(core * chunk, chunk), chunk)
    other = pl.ds(pl.multiple_of((1 - core) * chunk, chunk), chunk)
    sib_in = send(ac.at[half], ac.at[half], sems_c, 1, sibling)
    for copy in xa:
        copy.wait()

    col_half[0] = pack(jnp.dot(wat[other, :], ar[...], preferred_element_type=F32), occ)
    sib_out = send(col_half.at[0], sib_recv, sems_c, 2, sibling)
    sib_in.wait()

    xd = []
    for k in (1, 0, 2):
        theirs = pl.ds(pl.multiple_of((x ^ (k + 1)) * chunk, chunk), chunk)
        row_send[k] = pack(jnp.dot(w_v[theirs, :], ac[...], preferred_element_type=F32), occ)
        xd.append(send(row_send.at[k], x_recv.at[k], sems_d, k, x_peers[k]))
    own_cols = pack(jnp.dot(wat[half, :], ar[...], preferred_element_type=F32), occ)
    sib_out.wait()
    cross_send[...] = own_cols + sib_recv[...]
    cross_out = send(cross_send, cross_recv, sems_c, 3, source)
    own_rows = pack(jnp.dot(w_v[own_chunk, :], ac[...], preferred_element_type=F32), occ)
    for copy in xd:
        copy.wait()
    total = own_rows + x_recv[0] + x_recv[1] + x_recv[2]
    cross_out.wait()
    z_send[...] = total + cross_recv[...]

    ze = []
    for k in reversed(range(ZN - 1)):
        part = pl.ds(pl.multiple_of((zl ^ (k + 1)) * piece, piece), piece)
        ze.append(send(z_send.at[part], z_recv.at[k], sems_e, k, z_peers[k]))
    result = z_send[pl.ds(pl.multiple_of(zl * piece, piece), piece), :]
    for copy in ze:
        copy.wait()
    for k in range(ZN - 1):
        result = result + z_recv[k]
    out_ref[...] = unpack(result, occ)


def local(amplitudes, integrals, owner):
    occ, shard = amplitudes.shape
    rows, cols = integrals.shape
    chunk = rows // XN
    packed = chunk * 3 // 4
    dma = pltpu.SemaphoreType.DMA
    turned = pl.pallas_call(
        kernel,
        out_shape=jax.ShapeDtypeStruct((shard, LANES), F32),
        in_specs=[
            pl.BlockSpec(memory_space=pltpu.VMEM),
            pl.BlockSpec(memory_space=pl.ANY),
            pl.BlockSpec(memory_space=pl.ANY),
        ],
        out_specs=pl.BlockSpec(memory_space=pltpu.VMEM),
        scratch_shapes=[
            pltpu.VMEM((rows, cols), BF16),
            pltpu.VMEM((cols, rows), BF16),
            pltpu.SMEM((rows // TB, owner.shape[1]), jnp.int32),
            pltpu.VMEM((rows, LANES), BF16),
            pltpu.VMEM((cols, LANES), BF16),
            pltpu.VMEM((XN - 1, packed, LANES), F32),
            pltpu.VMEM((XN - 1, packed, LANES), F32),
            pltpu.VMEM((1, packed, LANES), F32),
            pltpu.VMEM((packed, LANES), F32),
            pltpu.VMEM((packed, LANES), F32),
            pltpu.VMEM((packed, LANES), F32),
            pltpu.VMEM((packed, LANES), F32),
            pltpu.VMEM((ZN - 1, packed // ZN, LANES), F32),
            dma,
            dma,
            dma((2, ZN - 1)),
            dma((2, XN - 1)),
            dma((2, 4)),
            dma((2, XN - 1)),
            dma((2, ZN - 1)),
        ],
        compiler_params=pltpu.CompilerParams(
            collective_id=0, has_side_effects=True, vmem_limit_bytes=24 * 1024 * 1024
        ),
    )(amplitudes, integrals, owner)
    return turned[:, :occ].T


def solution(mesh):
    in_specs = (P(None, ("row", "col")), P("row", "col"), P())
    out_specs = P(None, ("row", "col"))
    return jax.shard_map(local, mesh=mesh, in_specs=in_specs, out_specs=out_specs, check_vma=False)
```

time: 1900 us -> 54.8 us (0.03)
  the two profiles are of different devices: /device:TPU:1 before, /device:TPU:8 now
where the time goes in v1:
time: 54.8 us; the launch traced here: 54.6 us
  Pallas kernels  51.1 us (93%)
  local copies, waits for them, and re-layouts  3.47 us (6%)
    pallas_call x1, Pallas kernels, local(): pl.pallas_call(kernel, out_shape=jax.ShapeDtypeStruct((shard, LANES), F32...  51.1 us
    unnamed x5, local copies, waits for them, and re-layouts  2.86 us

profile of v1, /device:TPU:8, one launch (start us, length us, event | category | flops | bytes accessed | tf_op | source)
XLA Modules:
  0.0 54.6 jit_solution(13497051871066992478)
XLA Ops:
  0.0 0.8 %copy.4.amp_ref = bf16[96,32]{1,0:T(8,128)(2,1)S(1)} copy(bf16[96,32]{0,1:T(8,128)(2,1)} %param.3) | data formatting | bytes 12288 | tf_op args[0]
  0.8 0.0 copy-start
  0.8 1.2 %copy-done = bf16[1024,512]{1,0:T(8,128)(2,1)S(1)} copy-done((bf16[1024,512]{1,0:T(8,128)(2,1)S(1)}, bf16[1024,512]{1,0:T(8,128)(2,1)}, u32[]{:S(2)}) %copy-start) | copy-done | bytes 1048600
  2.0 0.0 copy-start.1
  2.0 0.8 %copy-done.1 = s32[128,128]{1,0:T(8,128)S(1)} copy-done((s32[128,128]{1,0:T(8,128)S(1)}, s32[128,128]{1,0:T(8,128)}, u32[]{:S(2)}) %copy-start.1) | copy-done | bytes 65560
  2.9 51.1 %shard_map.37 = f32[32,128]{1,0:T(8,128)S(1)} custom-call(bf16[96,32]{1,0:T(8,128)(2,1)S(1)} %copy.4.amp_ref, bf16[1024,512]{1,0:T(8,128)(2,1)S(1)} %copy-done, s32[128,128]{1,0:T(8,128)S(1)} %copy-done.1), custom_call_target="tpu_custom_call" | custom-call | tf_op jit(solution)/shard_map/pallas_call | solution.py:156
  54.0 0.6 %slice_bitcast_fusion = f32[96,32]{0,1:T(8,128)} fusion(f32[32,128]{1,0:T(8,128)S(1)} %shard_map.37), kind=kLoop, calls=%fused_computation | loop fusion | bytes 24576 | tf_op jit(solution)/shard_map/transpose | solution.py:191
Async XLA Ops:
  0.8 1.2 %copy-start = (bf16[1024,512]{1,0:T(8,128)(2,1)S(1)}, bf16[1024,512]{1,0:T(8,128)(2,1)}, u32[]{:S(2)}) copy-start(bf16[1024,512]{1,0:T(8,128)(2,1)} %w_hbm.1) | copy-start | bytes 3145732
  2.0 0.8 %copy-start.1 = (s32[128,128]{1,0:T(8,128)S(1)}, s32[128,128]{1,0:T(8,128)}, u32[]{:S(2)}) copy-start(s32[128,128]{1,0:T(8,128)} %owner_hbm.1) | copy-start | bytes 196612

commit v2 on v1

v2 whole, which is shorter than its diff:
```python
import jax
import jax.numpy as jnp
from jax import lax
from jax.experimental import pallas as pl
from jax.experimental.pallas import tpu as pltpu
from jax.sharding import PartitionSpec as P

TB = 128
LANES = 128
XN, YN, ZN, HN = 4, 4, 8, 2
MESH = pl.DeviceIdType.MESH
F32 = jnp.float32
BF16 = jnp.bfloat16


def pack(block, occ):
    lane = lax.broadcasted_iota(jnp.int32, (8, LANES), 1)
    out = []
    for s in range(block.shape[0] // 32):
        last = block[s * 32 + 24 : s * 32 + 32]
        for j in range(3):
            moved = pltpu.roll(last, occ - 32 * j, 1)
            out.append(jnp.where(lane < occ, block[s * 32 + 8 * j : s * 32 + 8 * j + 8], moved))
    return jnp.concatenate(out, axis=0)


def unpack(block, occ):
    lane = lax.broadcasted_iota(jnp.int32, (8, LANES), 1)
    last = jnp.zeros((8, LANES), F32)
    for j in range(3):
        moved = pltpu.roll(block[8 * j : 8 * j + 8], (LANES - occ + 32 * j) % LANES, 1)
        last = jnp.where((lane >= 32 * j) & (lane < 32 * j + 32), moved, last)
    return jnp.concatenate([block, last], axis=0)


def kernel(
    amp_hbm, w_hbm, owner_hbm, out_ref,
    amp_v, w_v, wat, own_s, ar, ac, row_send, x_recv, col_half, sib_recv, col_send, col_recv, z_send, z_recv,
    copy_sems, za_sems, xa_sems, ci_sems, sib_sems, co_sems, xd_sems, ze_sems,
):
    shard, occ = amp_v.shape
    rows, cols = w_v.shape
    row_tiles, col_tiles = rows // TB, cols // TB
    chunk = rows // XN
    packed = chunk * 3 // 4
    piece = packed // ZN
    r = lax.axis_index("row")
    c = lax.axis_index("col")
    y, zh, core = r // 4, (r // 2) % 2, r % 2
    x, zl = c // 8, c % 8

    def at(yy, zz, cc, xx, ll):
        return (yy * 4 + zz * 2 + cc, xx * 8 + ll)

    def rows_at(start, size, unit=8):
        return pl.ds(pl.multiple_of(start, unit), size)

    z_peers = [at(y, zh, core, x, zl ^ k) for k in range(1, ZN)]
    x_peers = [at(y, zh, core, x ^ k, zl) for k in range(1, XN)]
    sibling = at(y, zh, 1 - core, x, zl)
    spots = [(yy, hh) for hh in range(HN) for yy in range(YN)]
    reader_line = 4 * zh + 2 * core + x // 2
    readers = [at(yy, hh, x % 2, y, reader_line) for yy, hh in spots]
    writers = [at(x, zl // 4, (zl // 2) % 2, 2 * (zl % 2) + core, l) for l in range(ZN)]
    fixed = (x == y) & (core == x % 2) & (zl == reader_line)
    reads_self = [fixed & (y == yy) & (zh == hh) for yy, hh in spots]
    writes_self = [fixed & (zl == l) for l in range(ZN)]

    amp_copy = pltpu.make_async_copy(amp_hbm, amp_v, copy_sems.at[0])
    amp_copy.start()
    own_copy = pltpu.make_async_copy(owner_hbm.at[rows_at(r * row_tiles, row_tiles)], own_s, copy_sems.at[1])
    own_copy.start()
    w_copy = pltpu.make_async_copy(w_hbm, w_v, copy_sems.at[2])
    w_copy.start()

    barrier = pltpu.get_barrier_semaphore()

    def hello(peer):
        pl.semaphore_signal(barrier, inc=1, device_id=peer, device_id_type=MESH)

    for peer in z_peers + x_peers + [sibling]:
        hello(peer)
    for peer, own in zip(readers + writers, reads_self + writes_self):
        pl.when(jnp.logical_not(own))(lambda peer=peer: hello(peer))

    amp_copy.wait()
    mine = rows_at(x * chunk + zl * shard, shard, 32)
    ar[mine, :] = jnp.concatenate([amp_v[...], jnp.zeros((shard, LANES - occ), BF16)], axis=1)
    greeted = ZN - 1 + XN - 1 + 1 + len(readers) + len(writers)
    pl.semaphore_wait(barrier, greeted - 2 * fixed.astype(jnp.int32))

    def remote(src, dst, send_sem, recv_sem, peer):
        return pltpu.make_async_remote_copy(
            src_ref=src, dst_ref=dst, send_sem=send_sem, recv_sem=recv_sem, device_id=peer, device_id_type=MESH
        )

    def start(*args):
        copy = remote(*args)
        copy.start()
        return copy

    sent = []

    za = [None] * (ZN - 1)
    for k in reversed(range(ZN - 1)):
        za[k] = start(ar.at[mine], ar.at[mine], za_sems.at[0, k], za_sems.at[1, k], z_peers[k])
    sent += za
    ci_slot = rows_at((x % 2) * chunk + zl * shard, shard, 32)
    ci = []
    for k in range(len(spots)):
        copy = remote(ar.at[mine], ac.at[ci_slot], ci_sems.at[0, k], ci_sems.at[1, zl], readers[k])
        pl.when(jnp.logical_not(reads_self[k]))(copy.start)
        ci.append(copy)

    @pl.when(fixed)
    def _():
        pltpu.make_async_copy(ar.at[mine], ac.at[ci_slot], ci_sems.at[1, zl]).start()

    w_copy.wait()
    own_copy.wait()
    for i in range(row_tiles):
        for j in range(col_tiles):
            held = own_s[i, c * col_tiles + j] == 1
            tile = w_v[i * TB : (i + 1) * TB, j * TB : (j + 1) * TB]
            kept = jnp.where(held, tile, jnp.zeros_like(tile))
            w_v[i * TB : (i + 1) * TB, j * TB : (j + 1) * TB] = kept
            away = jnp.where(r * row_tiles + i == c * col_tiles + j, jnp.zeros_like(tile), kept)
            wat[j * TB : (j + 1) * TB, i * TB : (i + 1) * TB] = away.T

    groups = [(zl // 4 * 4, 4, (0, 1, 2)), ((zl ^ 4) // 2 * 2, 2, (3, 4)), ((zl ^ 6) // 2 * 2, 2, (5, 6))]
    xa = []
    for g, (first, count, waits) in enumerate(groups):
        for k in waits:
            za[k].wait_recv()
        part = rows_at(x * chunk + first * shard, count * shard, 32)
        for k in (1, 0, 2):
            xa.append(start(ar.at[part], ar.at[part], xa_sems.at[0, g, k], xa_sems.at[1, g, k], x_peers[k]))
    sent += xa

    half = rows_at(core * chunk, chunk, 256)
    other = rows_at((1 - core) * chunk, chunk, 256)
    for copy in xa:
        copy.wait_recv()

    col_half[...] = pack(jnp.dot(wat[other, :], ar[...], preferred_element_type=F32), occ)
    sib_out = start(col_half, sib_recv, sib_sems.at[0, 1], sib_sems.at[1, 1], sibling)

    for l in range(ZN):
        slot = rows_at(core * chunk + l * shard, shard, 32)
        remote(ar.at[mine], ac.at[slot], ci_sems.at[0, 0], ci_sems.at[1, l], sibling).wait_recv()
    sib_in = start(ac.at[half], ac.at[half], sib_sems.at[0, 0], sib_sems.at[1, 0], sibling)
    own_cols = pack(jnp.dot(wat[half, :], ar[...], preferred_element_type=F32), occ)
    sib_out.wait_recv()
    col_send[...] = own_cols + sib_recv[...]
    co = []
    for l in range(ZN):
        part = pl.ds(l * piece, piece)
        copy = remote(col_send.at[part], col_recv.at[zh * YN + y], co_sems.at[0, l], co_sems.at[1, zh * YN + y], writers[l])
        pl.when(jnp.logical_not(writes_self[l]))(copy.start)
        co.append(copy)

    @pl.when(fixed)
    def _():
        pltpu.make_async_copy(
            col_send.at[rows_at(zl * piece, piece)], col_recv.at[zh * YN + y], co_sems.at[1, zh * YN + y]
        ).start()

    sib_in.wait_recv()
    outs = list(reversed(groups))
    xd = [[None] * (XN - 1) for _ in outs]

    def leave(g, k):
        first, count, _ = outs[g]
        part = rows_at(first * piece, count * piece)
        xd[g][k] = start(
            row_send.at[k, part], x_recv.at[k, part], xd_sems.at[0, g, k], xd_sems.at[1, g, k], x_peers[k]
        )

    for k in (1, 0, 2):
        theirs = rows_at((x ^ (k + 1)) * chunk, chunk, 256)
        row_send[k] = pack(jnp.dot(w_v[theirs, :], ac[...], preferred_element_type=F32), occ)
        leave(0, k)
    for g in range(1, len(outs)):
        for k in (1, 0, 2):
            leave(g, k)
    z_send[...] = pack(jnp.dot(w_v[rows_at(x * chunk, chunk, 256), :], ac[...], preferred_element_type=F32), occ)

    ze = []
    for g, (first, count, waits) in enumerate(outs):
        for copy in xd[g]:
            copy.wait_recv()
        part = rows_at(first * piece, count * piece)
        total = z_send[part, :]
        for k in range(XN - 1):
            total = total + x_recv[k, part, :]
        z_send[part, :] = total
        for k in reversed(waits):
            where = rows_at((zl ^ (k + 1)) * piece, piece)
            ze.append(start(z_send.at[where], z_recv.at[k], ze_sems.at[0, k], ze_sems.at[1, k], z_peers[k]))
    sent += [copy for line in xd for copy in line] + ze + [sib_in, sib_out]

    result = z_send[rows_at(zl * piece, piece), :]
    for copy in ze:
        copy.wait_recv()
    for k in range(ZN - 1):
        result = result + z_recv[k]
    for k in range(len(spots)):
        part = pl.ds(0, piece)
        remote(col_send.at[part], col_recv.at[k], co_sems.at[0, 0], co_sems.at[1, k], sibling).wait_recv()
    for k in range(len(spots)):
        result = result + col_recv[k]
    out_ref[...] = unpack(result, occ)[:, :occ]

    for copy in sent:
        copy.wait_send()
    for copies, own in ((ci, reads_self), (co, writes_self)):
        for copy, to_self in zip(copies, own):
            pl.when(jnp.logical_not(to_self))(copy.wait_send)


def local(amplitudes, integrals, owner):
    occ, shard = amplitudes.shape
    rows, cols = integrals.shape
    packed = rows // XN * 3 // 4
    piece = packed // ZN
    dma = pltpu.SemaphoreType.DMA
    hbm = pl.BlockSpec(memory_space=pltpu.HBM)
    turned = pl.pallas_call(
        kernel,
        out_shape=jax.ShapeDtypeStruct((shard, occ), F32),
        in_specs=[hbm, hbm, hbm],
        out_specs=pl.BlockSpec(memory_space=pltpu.VMEM),
        scratch_shapes=[
            pltpu.VMEM((shard, occ), BF16),
            pltpu.VMEM((rows, cols), BF16),
            pltpu.VMEM((cols, rows), BF16),
            pltpu.SMEM((rows // TB, owner.shape[1]), jnp.int32),
            pltpu.VMEM((rows, LANES), BF16),
            pltpu.VMEM((cols, LANES), BF16),
            pltpu.VMEM((XN - 1, packed, LANES), F32),
            pltpu.VMEM((XN - 1, packed, LANES), F32),
            pltpu.VMEM((packed, LANES), F32),
            pltpu.VMEM((packed, LANES), F32),
            pltpu.VMEM((packed, LANES), F32),
            pltpu.VMEM((YN * HN, piece, LANES), F32),
            pltpu.VMEM((packed, LANES), F32),
            pltpu.VMEM((ZN - 1, piece, LANES), F32),
            dma((3,)),
            dma((2, ZN - 1)),
            dma((2, 3, XN - 1)),
            dma((2, ZN)),
            dma((2, 2)),
            dma((2, ZN)),
            dma((2, 3, XN - 1)),
            dma((2, ZN - 1)),
        ],
        compiler_params=pltpu.CompilerParams(
            collective_id=0, has_side_effects=True, vmem_limit_bytes=16 * 1024 * 1024
        ),
    )(amplitudes.T, integrals, owner)
    return turned.T


def solution(mesh):
    in_specs = (P(None, ("row", "col")), P("row", "col"), P())
    out_specs = P(None, ("row", "col"))
    return jax.shard_map(local, mesh=mesh, in_specs=in_specs, out_specs=out_specs, check_vma=False)
```

time: 54.8 us -> 50.1 us (0.914)
  the two profiles are of different devices: /device:TPU:8 before, /device:TPU:1 now
where the time goes in v2:
time: 50.1 us; the launch traced here: 49.9 us
  Pallas kernels  46.5 us (93%)
  local copies, waits for them, and re-layouts  3.37 us (7%)
    pallas_call x1, Pallas kernels, local(): pl.pallas_call(kernel, out_shape=jax.ShapeDtypeStruct((shard, occ), F32),...  46.5 us
    unnamed x7, local copies, waits for them, and re-layouts  3.37 us

profile of v2, /device:TPU:1, one launch (start us, length us, event | category | flops | bytes accessed | tf_op | source)
XLA Modules:
  0.0 49.9 jit_solution(3252583014032912836)
XLA Ops:
  0.0 0.0 copy-start
  0.0 1.2 %copy-done = bf16[1024,512]{1,0:T(8,128)(2,1)S(1)} copy-done((bf16[1024,512]{1,0:T(8,128)(2,1)S(1)}, bf16[1024,512]{1,0:T(8,128)(2,1)}, u32[]{:S(2)}) %copy-start) | copy-done | bytes 1048600
  1.2 0.0 copy-start.1
  1.2 0.8 %copy-done.1 = s32[128,128]{1,0:T(8,128)S(1)} copy-done((s32[128,128]{1,0:T(8,128)S(1)}, s32[128,128]{1,0:T(8,128)}, u32[]{:S(2)}) %copy-start.1) | copy-done | bytes 65560
  2.1 0.0 copy-start.2
  2.1 0.7 %copy-done.2 = bf16[96,32]{0,1:T(8,128)(2,1)S(1)} copy-done((bf16[96,32]{0,1:T(8,128)(2,1)S(1)}, bf16[96,32]{0,1:T(8,128)(2,1)}, u32[]{:S(2)}) %copy-start.2) | copy-done | bytes 6168
  2.8 46.5 %shard_map.37 = f32[32,96]{1,0:T(8,128)S(1)} custom-call(bf16[32,96]{1,0:T(8,128)(2,1)S(1)} %bitcast.3, bf16[1024,512]{1,0:T(8,128)(2,1)S(1)} %copy-done, s32[128,128]{1,0:T(8,128)S(1)} %copy-done.1), custom_call_target="tpu_custom_call" | custom-call | tf_op jit(solution)/shard_map/pallas_call | solution.py:228
  49.3 0.6 %copy.5 = f32[96,32]{0,1:T(8,128)} copy(f32[96,32]{0,1:T(8,128)S(1)} %bitcast.2) | data formatting | bytes 24576
Async XLA Ops:
  0.0 1.2 %copy-start = (bf16[1024,512]{1,0:T(8,128)(2,1)S(1)}, bf16[1024,512]{1,0:T(8,128)(2,1)}, u32[]{:S(2)}) copy-start(bf16[1024,512]{1,0:T(8,128)(2,1)} %w_hbm.1) | copy-start | bytes 3145732
  1.2 0.8 %copy-start.1 = (s32[128,128]{1,0:T(8,128)S(1)}, s32[128,128]{1,0:T(8,128)}, u32[]{:S(2)}) copy-start(s32[128,128]{1,0:T(8,128)} %owner_hbm.1) | copy-start | bytes 196612
  2.1 0.7 %copy-start.2 = (bf16[96,32]{0,1:T(8,128)(2,1)S(1)}, bf16[96,32]{0,1:T(8,128)(2,1)}, u32[]{:S(2)}) copy-start(bf16[96,32]{0,1:T(8,128)(2,1)} %param.3) | copy-start | bytes 18436

commit v3 on v2

v3 whole, which is shorter than its diff:
```python
import jax
import jax.numpy as jnp
from jax import lax
from jax.experimental import pallas as pl
from jax.experimental.pallas import tpu as pltpu
from jax.sharding import PartitionSpec as P

TB = 128
LANES = 128
XN, YN, ZN, HN = 4, 4, 8, 2
MESH = pl.DeviceIdType.MESH
F32 = jnp.float32
BF16 = jnp.bfloat16


def pack(block, occ):
    lane = lax.broadcasted_iota(jnp.int32, (8, LANES), 1)
    out = []
    for s in range(block.shape[0] // 32):
        last = block[s * 32 + 24 : s * 32 + 32]
        for j in range(3):
            moved = pltpu.roll(last, occ - 32 * j, 1)
            out.append(jnp.where(lane < occ, block[s * 32 + 8 * j : s * 32 + 8 * j + 8], moved))
    return jnp.concatenate(out, axis=0)


def unpack(block, occ):
    lane = lax.broadcasted_iota(jnp.int32, (8, LANES), 1)
    last = jnp.zeros((8, LANES), F32)
    for j in range(3):
        moved = pltpu.roll(block[8 * j : 8 * j + 8], (LANES - occ + 32 * j) % LANES, 1)
        last = jnp.where((lane >= 32 * j) & (lane < 32 * j + 32), moved, last)
    return jnp.concatenate([block, last], axis=0)


def kernel(
    amp_hbm, w_hbm, owner_hbm, out_ref,
    amp_v, w_v, wat, own_s, ar, ac, row_send, x_recv, col_all, team_recv, col_send, col_recv, z_send, z_recv,
    copy_sems, za_sems, xa_sems, ci_sems, ga_sems, gd_sems, co_sems, xd_sems, ze_sems,
):
    shard, occ = amp_v.shape
    rows, cols = w_v.shape
    row_tiles, col_tiles = rows // TB, cols // TB
    chunk = rows // XN
    packed = chunk * 3 // 4
    piece = packed // ZN
    r = lax.axis_index("row")
    c = lax.axis_index("col")
    y, zh, core = r // 4, (r // 2) % 2, r % 2
    x, zl = c // 8, c % 8

    def at(yy, zz, cc, xx, ll):
        return (yy * 4 + zz * 2 + cc, xx * 8 + ll)

    def rows_at(start, size, unit=8):
        return pl.ds(pl.multiple_of(start, unit), size)

    z_peers = [at(y, zh, core, x, zl ^ k) for k in range(1, ZN)]
    x_peers = [at(y, zh, core, x ^ k, zl) for k in range(1, XN)]
    mates = [(y ^ (m // 2), core ^ (m % 2)) for m in range(1, 2 * YN)]
    team = [at(yy, zh, cc, x, zl) for yy, cc in mates]
    pair = y ^ 1
    readers = [at((zl // 2) ^ 1, hh, x % 2, y, 4 * zh + 2 * core + x // 2) for hh in range(HN)]
    writers = [at(x, zl // 4, (zl // 2) % 2, 2 * (zl % 2) + core, 2 * pair + l) for l in range(2)]

    barrier = pltpu.get_barrier_semaphore()
    greeted = writers + z_peers[::-1] + team[::-1] + x_peers
    for peer in greeted:
        pl.semaphore_signal(barrier, inc=1, device_id=peer, device_id_type=MESH)

    amp_copy = pltpu.make_async_copy(amp_hbm, amp_v, copy_sems.at[0])
    amp_copy.start()
    own_copy = pltpu.make_async_copy(owner_hbm.at[rows_at(r * row_tiles, row_tiles)], own_s, copy_sems.at[1])
    own_copy.start()
    w_copy = pltpu.make_async_copy(w_hbm, w_v, copy_sems.at[2])
    w_copy.start()

    amp_copy.wait()
    mine = rows_at(x * chunk + zl * shard, shard, 32)
    ar[mine, :] = jnp.concatenate([amp_v[...], jnp.zeros((shard, LANES - occ), BF16)], axis=1)
    pl.semaphore_wait(barrier, len(greeted))

    def remote(src, dst, send_sem, recv_sem, peer):
        return pltpu.make_async_remote_copy(
            src_ref=src, dst_ref=dst, send_sem=send_sem, recv_sem=recv_sem, device_id=peer, device_id_type=MESH
        )

    sent = []

    def start(*args):
        copy = remote(*args)
        copy.start()
        sent.append(copy)
        return copy

    za = [None] * (ZN - 1)
    slot = rows_at((x % 2) * chunk + zl * shard, shard, 32)

    def to_line():
        for k in reversed(range(ZN - 1)):
            za[k] = start(ar.at[mine], ar.at[mine], za_sems.at[0, k], za_sems.at[1, k], z_peers[k])

    def to_readers():
        for k in range(HN):
            start(ar.at[mine], ac.at[slot], ci_sems.at[0, k], ci_sems.at[1, zl % 2], readers[k])

    to_readers()
    to_line()

    w_copy.wait()
    own_copy.wait()
    for i in range(row_tiles):
        for j in range(col_tiles):
            held = own_s[i, c * col_tiles + j] == 1
            tile = w_v[i * TB : (i + 1) * TB, j * TB : (j + 1) * TB]
            kept = jnp.where(held, tile, jnp.zeros_like(tile))
            w_v[i * TB : (i + 1) * TB, j * TB : (j + 1) * TB] = kept
            away = jnp.where(r * row_tiles + i == c * col_tiles + j, jnp.zeros_like(tile), kept)
            wat[j * TB : (j + 1) * TB, i * TB : (i + 1) * TB] = away.T

    groups = [(zl // 4 * 4, 4, (0, 1, 2)), ((zl ^ 4) // 2 * 2, 2, (3, 4)), ((zl ^ 6) // 2 * 2, 2, (5, 6))]
    xa = []
    for g, (first, count, waits) in enumerate(groups):
        for k in waits:
            za[k].wait_recv()
        part = rows_at(x * chunk + first * shard, count * shard, 32)
        for k in (1, 0, 2):
            xa.append(start(ar.at[part], ar.at[part], xa_sems.at[0, g, k], xa_sems.at[1, g, k], x_peers[k]))

    fetched = rows_at(core * chunk + pair * 2 * shard, 2 * shard, 64)

    def share():
        for l in range(2):
            remote(ar.at[mine], ac.at[slot], ci_sems.at[0, 0], ci_sems.at[1, l], writers[l]).wait_recv()
        return [
            start(ac.at[fetched], ac.at[fetched], ga_sems.at[0, m], ga_sems.at[1, m], team[m])
            for m in reversed(range(len(team)))
        ]

    outs = list(reversed(groups))
    xd = [[None] * (XN - 1) for _ in outs]

    def leave(g, k):
        first, count, _ = outs[g]
        part = rows_at(first * piece, count * piece)
        xd[g][k] = start(
            row_send.at[k, part], x_recv.at[k, part], xd_sems.at[0, g, k], xd_sems.at[1, g, k], x_peers[k]
        )

    def row_terms():
        for k in (1, 0, 2):
            theirs = rows_at((x ^ (k + 1)) * chunk, chunk, 256)
            row_send[k] = pack(jnp.dot(w_v[theirs, :], ac[...], preferred_element_type=F32), occ)
            leave(0, k)
        for g in range(1, len(outs)):
            for k in (1, 0, 2):
                leave(g, k)

    def own_rows():
        z_send[...] = pack(jnp.dot(w_v[rows_at(x * chunk, chunk, 256), :], ac[...], preferred_element_type=F32), occ)

    def col_terms():
        col_all[...] = pack(jnp.dot(wat[...], ar[...], preferred_element_type=F32), occ)
        out = []
        for m in reversed(range(len(team))):
            yy, cc = mates[m]
            part = rows_at(cc * packed + (yy ^ 1) * 2 * piece, 2 * piece)
            out.append(start(col_all.at[part], team_recv.at[m], gd_sems.at[0, m], gd_sems.at[1, m], team[m]))
        return out

    def col_out():
        for copy in gd:
            copy.wait_recv()
        total = col_all[rows_at(core * packed + pair * 2 * piece, 2 * piece), :]
        for m in range(len(team)):
            total = total + team_recv[m]
        col_send[...] = total
        for l in range(2):
            part = pl.ds(l * piece, piece)
            start(col_send.at[part], col_recv.at[zh], co_sems.at[0, l], co_sems.at[1, zh], writers[l])

    def all_in(copies):
        for copy in copies:
            copy.wait_recv()

    ga = share()
    all_in(xa)
    gd = col_terms()
    all_in(ga)
    row_terms()
    own_rows()
    col_out()

    ze = []
    for g, (first, count, waits) in enumerate(outs):
        all_in(xd[g])
        part = rows_at(first * piece, count * piece)
        total = z_send[part, :]
        for k in range(XN - 1):
            total = total + x_recv[k, part, :]
        z_send[part, :] = total
        for k in reversed(waits):
            where = rows_at((zl ^ (k + 1)) * piece, piece)
            ze.append(start(z_send.at[where], z_recv.at[k], ze_sems.at[0, k], ze_sems.at[1, k], z_peers[k]))

    result = z_send[rows_at(zl * piece, piece), :]
    all_in(ze)
    for k in range(ZN - 1):
        result = result + z_recv[k]
    for h in range(HN):
        remote(col_send.at[pl.ds(0, piece)], col_recv.at[h], co_sems.at[0, 0], co_sems.at[1, h], readers[h]).wait_recv()
    for h in range(HN):
        result = result + col_recv[h]
    out_ref[...] = unpack(result, occ)[:, :occ]

    for copy in sent:
        copy.wait_send()


def local(amplitudes, integrals, owner):
    occ, shard = amplitudes.shape
    rows, cols = integrals.shape
    packed = rows // XN * 3 // 4
    piece = packed // ZN
    dma = pltpu.SemaphoreType.DMA
    hbm = pl.BlockSpec(memory_space=pltpu.HBM)
    turned = pl.pallas_call(
        kernel,
        out_shape=jax.ShapeDtypeStruct((shard, occ), F32),
        in_specs=[hbm, hbm, hbm],
        out_specs=pl.BlockSpec(memory_space=pltpu.VMEM),
        scratch_shapes=[
            pltpu.VMEM((shard, occ), BF16),
            pltpu.VMEM((rows, cols), BF16),
            pltpu.VMEM((cols, rows), BF16),
            pltpu.SMEM((rows // TB, owner.shape[1]), jnp.int32),
            pltpu.VMEM((rows, LANES), BF16),
            pltpu.VMEM((cols, LANES), BF16),
            pltpu.VMEM((XN - 1, packed, LANES), F32),
            pltpu.VMEM((XN - 1, packed, LANES), F32),
            pltpu.VMEM((2 * packed, LANES), F32),
            pltpu.VMEM((2 * YN - 1, 2 * piece, LANES), F32),
            pltpu.VMEM((2 * piece, LANES), F32),
            pltpu.VMEM((HN, piece, LANES), F32),
            pltpu.VMEM((packed, LANES), F32),
            pltpu.VMEM((ZN - 1, piece, LANES), F32),
            dma((3,)),
            dma((2, ZN - 1)),
            dma((2, 3, XN - 1)),
            dma((2, 2)),
            dma((2, 2 * YN - 1)),
            dma((2, 2 * YN - 1)),
            dma((2, 2)),
            dma((2, 3, XN - 1)),
            dma((2, ZN - 1)),
        ],
        compiler_params=pltpu.CompilerParams(
            collective_id=0, has_side_effects=True, vmem_limit_bytes=56 * 1024 * 1024
        ),
    )(amplitudes.T, integrals, owner)
    return turned.T


def solution(mesh):
    in_specs = (P(None, ("row", "col")), P("row", "col"), P())
    out_specs = P(None, ("row", "col"))
    return jax.shard_map(local, mesh=mesh, in_specs=in_specs, out_specs=out_specs, check_vma=False)
```

time: 50.1 us -> 44.5 us (0.89)
  the two profiles are of different devices: /device:TPU:1 before, /device:TPU:2 now
where the time goes in v3:
time: 44.5 us; the launch traced here: 44.2 us
  Pallas kernels  42.9 us (96%)
  local copies, waits for them, and re-layouts  1.32 us (3%)
    pallas_call x1, Pallas kernels, local(): pl.pallas_call(kernel, out_shape=jax.ShapeDtypeStruct((shard, occ), F32),...  42.9 us
    unnamed x1, local copies, waits for them, and re-layouts  1.32 us

profile of v3, /device:TPU:2, one launch (start us, length us, event | category | flops | bytes accessed | tf_op | source)
XLA Modules:
  0.0 44.2 jit_solution(8283938490520803221)
XLA Ops:
  0.0 42.9 %shard_map.37 = f32[32,96]{1,0:T(8,128)} custom-call(bf16[32,96]{1,0:T(8,128)(2,1)} %bitcast.3, bf16[1024,512]{1,0:T(8,128)(2,1)} %w_hbm.1, s32[128,128]{1,0:T(8,128)} %owner_hbm.1), custom_call_target="tpu_custom_call" | custom-call | tf_op jit(solution)/shard_map/pallas_call | solution.py:227
  42.9 1.3 %copy.5 = f32[96,32]{0,1:T(8,128)} copy(f32[96,32]{0,1:T(8,128)} %bitcast.2) | data formatting | bytes 24576

commit v4 on v3

--- a/solution.py
+++ b/solution.py
@@ -36,7 +36,7 @@
 def kernel(
     amp_hbm, w_hbm, owner_hbm, out_ref,
     amp_v, w_v, wat, own_s, ar, ac, row_send, x_recv, col_all, team_recv, col_send, col_recv, z_send, z_recv,
-    copy_sems, za_sems, xa_sems, ci_sems, ga_sems, gd_sems, co_sems, xd_sems, ze_sems,
+    copy_sems, za_sems, xa_sems, ci_sems, ga_sems, gd_sems, co_sems, xd_sems, ze_sems, ready,
 ):
     shard, occ = amp_v.shape
     rows, cols = w_v.shape
@@ -59,14 +59,32 @@
     x_peers = [at(y, zh, core, x ^ k, zl) for k in range(1, XN)]
     mates = [(y ^ (m // 2), core ^ (m % 2)) for m in range(1, 2 * YN)]
     team = [at(yy, zh, cc, x, zl) for yy, cc in mates]
-    pair = y ^ 1
-    readers = [at((zl // 2) ^ 1, hh, x % 2, y, 4 * zh + 2 * core + x // 2) for hh in range(HN)]
+
+    def pair_of(yy):
+        return (zl // 2) ^ ((yy - x) % 4) ^ jnp.where(zh == zl // 4, 3, 0)
+
+    pair = pair_of(y)
+
+    def reader(hh):
+        line = 4 * zh + 2 * core + x // 2
+        turn = (zl // 2) ^ (line // 2) ^ jnp.where(zh == hh, 3, 0)
+        return at((y + turn) % 4, hh, x % 2, y, line)
+
+    readers = [reader(hh) for hh in range(HN)]
     writers = [at(x, zl // 4, (zl // 2) % 2, 2 * (zl % 2) + core, 2 * pair + l) for l in range(2)]
 
     barrier = pltpu.get_barrier_semaphore()
-    greeted = writers + z_peers[::-1] + team[::-1] + x_peers
-    for peer in greeted:
-        pl.semaphore_signal(barrier, inc=1, device_id=peer, device_id_type=MESH)
+    ahead = zh == 0
+    answering = (zh == 1) & (zl // 4 == 0)
+
+    def greet(peers):
+        for peer in peers:
+            pl.semaphore_signal(barrier, inc=1, device_id=peer, device_id_type=MESH)
+
+    pl.when(jnp.logical_not(answering))(lambda: greet(writers))
+    pl.when(ahead)(lambda: greet(readers[1:]))
+    always = z_peers[::-1] + team[::-1] + x_peers
+    greet(always)
 
     amp_copy = pltpu.make_async_copy(amp_hbm, amp_v, copy_sems.at[0])
     amp_copy.start()
@@ -78,7 +96,12 @@
     amp_copy.wait()
     mine = rows_at(x * chunk + zl * shard, shard, 32)
     ar[mine, :] = jnp.concatenate([amp_v[...], jnp.zeros((shard, LANES - occ), BF16)], axis=1)
-    pl.semaphore_wait(barrier, len(greeted))
+    pl.semaphore_wait(barrier, len(always) + HN - ahead.astype(jnp.int32) + 2 * answering.astype(jnp.int32))
+
+    @pl.when(answering)
+    def _():
+        for peer in writers:
+            pl.semaphore_signal(ready, inc=1, device_id=peer, device_id_type=MESH)
 
     def remote(src, dst, send_sem, recv_sem, peer):
         return pltpu.make_async_remote_copy(
@@ -100,11 +123,12 @@
         for k in reversed(range(ZN - 1)):
             za[k] = start(ar.at[mine], ar.at[mine], za_sems.at[0, k], za_sems.at[1, k], z_peers[k])
 
-    def to_readers():
-        for k in range(HN):
-            start(ar.at[mine], ac.at[slot], ci_sems.at[0, k], ci_sems.at[1, zl % 2], readers[k])
-
-    to_readers()
+    ci = [
+        remote(ar.at[mine], ac.at[slot], ci_sems.at[0, k], ci_sems.at[1, zl % 2], readers[k]) for k in range(HN)
+    ]
+    sent += ci
+    ci[0].start()
+    pl.when(jnp.logical_not(ahead))(ci[1].start)
     to_line()
 
     w_copy.wait()
@@ -129,13 +153,18 @@
 
     fetched = rows_at(core * chunk + pair * 2 * shard, 2 * shard, 64)
 
+    def answer():
+        pl.semaphore_wait(ready, 1)
+        ci[1].start()
+
+    ga = [remote(ac.at[fetched], ac.at[fetched], ga_sems.at[0, m], ga_sems.at[1, m], team[m]) for m in range(len(team))]
+    sent += ga
+
     def share():
         for l in range(2):
             remote(ar.at[mine], ac.at[slot], ci_sems.at[0, 0], ci_sems.at[1, l], writers[l]).wait_recv()
-        return [
-            start(ac.at[fetched], ac.at[fetched], ga_sems.at[0, m], ga_sems.at[1, m], team[m])
-            for m in reversed(range(len(team)))
-        ]
+        for copy in reversed(ga):
+            copy.start()
 
     outs = list(reversed(groups))
     xd = [[None] * (XN - 1) for _ in outs]
@@ -164,7 +193,7 @@
         out = []
         for m in reversed(range(len(team))):
             yy, cc = mates[m]
-            part = rows_at(cc * packed + (yy ^ 1) * 2 * piece, 2 * piece)
+            part = rows_at(cc * packed + pair_of(yy) * 2 * piece, 2 * piece)
             out.append(start(col_all.at[part], team_recv.at[m], gd_sems.at[0, m], gd_sems.at[1, m], team[m]))
         return out
 
@@ -175,21 +204,32 @@
         for m in range(len(team)):
             total = total + team_recv[m]
         col_send[...] = total
-        for l in range(2):
-            part = pl.ds(l * piece, piece)
-            start(col_send.at[part], col_recv.at[zh], co_sems.at[0, l], co_sems.at[1, zh], writers[l])
+        for copy in co:
+            copy.start()
+
+    co = [
+        remote(
+            col_send.at[pl.ds(l * piece, piece)], col_recv.at[zh], co_sems.at[0, l], co_sems.at[1, zh], writers[l]
+        )
+        for l in range(2)
+    ]
+    sent += co
 
     def all_in(copies):
         for copy in copies:
             copy.wait_recv()
 
-    ga = share()
+    behind = jnp.logical_not(ahead)
+    pl.when(ahead)(answer)
+    pl.when(ahead)(share)
     all_in(xa)
     gd = col_terms()
+    pl.when(behind)(col_out)
+    pl.when(behind)(share)
     all_in(ga)
     row_terms()
+    pl.when(ahead)(col_out)
     own_rows()
-    col_out()
 
     ze = []
     for g, (first, count, waits) in enumerate(outs):
@@ -253,6 +293,7 @@
             dma((2, 2)),
             dma((2, 3, XN - 1)),
             dma((2, ZN - 1)),
+            pltpu.SemaphoreType.REGULAR,
         ],
         compiler_params=pltpu.CompilerParams(
             collective_id=0, has_side_effects=True, vmem_limit_bytes=56 * 1024 * 1024

time: 44.5 us -> 43.4 us (0.975)
  the two profiles are of different devices: /device:TPU:2 before, /device:TPU:8 now
where the time goes in v4:
time: 43.4 us; the launch traced here: 43.1 us
  Pallas kernels  41.8 us (96%)
  local copies, waits for them, and re-layouts  1.32 us (3%)
    pallas_call x1, Pallas kernels, local(): pl.pallas_call(kernel, out_shape=jax.ShapeDtypeStruct((shard, occ), F32),...  41.8 us
    unnamed x1, local copies, waits for them, and re-layouts  1.32 us

profile of v4, /device:TPU:8, one launch (start us, length us, event | category | flops | bytes accessed | tf_op | source)
XLA Modules:
  0.0 43.1 jit_solution(10485355416651848950)
XLA Ops:
  0.0 41.8 %shard_map.37 = f32[32,96]{1,0:T(8,128)} custom-call(bf16[32,96]{1,0:T(8,128)(2,1)} %bitcast.3, bf16[1024,512]{1,0:T(8,128)(2,1)} %w_hbm.1, s32[128,128]{1,0:T(8,128)} %owner_hbm.1), custom_call_target="tpu_custom_call" | custom-call | tf_op jit(solution)/shard_map/pallas_call | solution.py:267
  41.8 1.3 %copy.5 = f32[96,32]{0,1:T(8,128)} copy(f32[96,32]{0,1:T(8,128)} %bitcast.2) | data formatting | bytes 24576

commit v5 on v4

--- a/solution.py
+++ b/solution.py
@@ -266,7 +266,7 @@
     hbm = pl.BlockSpec(memory_space=pltpu.HBM)
     turned = pl.pallas_call(
         kernel,
-        out_shape=jax.ShapeDtypeStruct((shard, occ), F32),
+        out_shape=pltpu.VMEM((shard, occ), F32),
         in_specs=[hbm, hbm, hbm],
         out_specs=pl.BlockSpec(memory_space=pltpu.VMEM),
         scratch_shapes=[

time: 43.4 us -> 42 us (0.968)
  local copies, waits for them, and re-layouts: 1.32 us -> 0.61 us
  Pallas kernels: 41.8 us -> 41.2 us
    unnamed x1, local copies, waits for them, and re-layouts: 1.32 us -> 0.61 us
    pallas_call x1, Pallas kernels: 41.8 us -> 41.2 us  [local(): pl.pallas_call(kernel, out_shape=pltpu.VMEM((shard, occ), F32), in_specs=...]
where the time goes in v5:
time: 42 us; the launch traced here: 41.8 us
  Pallas kernels  41.2 us (98%)
  local copies, waits for them, and re-layouts  0.61 us (1%)
    pallas_call x1, Pallas kernels, local(): pl.pallas_call(kernel, out_shape=pltpu.VMEM((shard, occ), F32), in_specs=...  41.2 us

profile of v5, /device:TPU:8, one launch (start us, length us, event | category | flops | bytes accessed | tf_op | source)
XLA Modules:
  0.0 41.8 jit_solution(15825531893321463933)
XLA Ops:
  0.0 41.2 %shard_map.37 = f32[32,96]{1,0:T(8,128)S(1)} custom-call(bf16[32,96]{1,0:T(8,128)(2,1)} %bitcast.3, bf16[1024,512]{1,0:T(8,128)(2,1)} %w_hbm.1, s32[128,128]{1,0:T(8,128)} %owner_hbm.1), custom_call_target="tpu_custom_call" | custom-call | tf_op jit(solution)/shard_map/pallas_call | solution.py:267
  41.2 0.6 %copy.5 = f32[96,32]{0,1:T(8,128)} copy(f32[96,32]{0,1:T(8,128)S(1)} %bitcast.2) | data formatting | bytes 24576

commit v6 on v5

--- a/solution.py
+++ b/solution.py
@@ -166,7 +166,7 @@
         for copy in reversed(ga):
             copy.start()
 
-    outs = list(reversed(groups))
+    outs = [(zl ^ q, 1, (q - 1,)) for q in (7, 6, 5, 4)] + [groups[0]]
     xd = [[None] * (XN - 1) for _ in outs]
 
     def leave(g, k):
@@ -291,7 +291,7 @@
             dma((2, 2 * YN - 1)),
             dma((2, 2 * YN - 1)),
             dma((2, 2)),
-            dma((2, 3, XN - 1)),
+            dma((2, 5, XN - 1)),
             dma((2, ZN - 1)),
             pltpu.SemaphoreType.REGULAR,
         ],

time: 42 us -> 41.6 us (level)
  the two profiles are of different devices: /device:TPU:8 before, /device:TPU:1 now
where the time goes in v6:
time: 41.6 us; the launch traced here: 41.4 us
  Pallas kernels  40.8 us (98%)
  local copies, waits for them, and re-layouts  0.61 us (1%)
    pallas_call x1, Pallas kernels, local(): pl.pallas_call(kernel, out_shape=pltpu.VMEM((shard, occ), F32), in_specs=...  40.8 us

profile of v6, /device:TPU:1, one launch (start us, length us, event | category | flops | bytes accessed | tf_op | source)
XLA Modules:
  0.0 41.4 jit_solution(16245074957865400833)
XLA Ops:
  0.0 40.8 %shard_map.37 = f32[32,96]{1,0:T(8,128)S(1)} custom-call(bf16[32,96]{1,0:T(8,128)(2,1)} %bitcast.3, bf16[1024,512]{1,0:T(8,128)(2,1)} %w_hbm.1, s32[128,128]{1,0:T(8,128)} %owner_hbm.1), custom_call_target="tpu_custom_call" | custom-call | tf_op jit(solution)/shard_map/pallas_call | solution.py:267
  40.8 0.6 %copy.5 = f32[96,32]{0,1:T(8,128)} copy(f32[96,32]{0,1:T(8,128)S(1)} %bitcast.2) | data formatting | bytes 24576

commit v7 on v6

--- a/solution.py
+++ b/solution.py
@@ -73,25 +73,25 @@
     readers = [reader(hh) for hh in range(HN)]
     writers = [at(x, zl // 4, (zl // 2) % 2, 2 * (zl % 2) + core, 2 * pair + l) for l in range(2)]
 
-    barrier = pltpu.get_barrier_semaphore()
-    ahead = zh == 0
-    answering = (zh == 1) & (zl // 4 == 0)
-
-    def greet(peers):
-        for peer in peers:
-            pl.semaphore_signal(barrier, inc=1, device_id=peer, device_id_type=MESH)
-
-    pl.when(jnp.logical_not(answering))(lambda: greet(writers))
-    pl.when(ahead)(lambda: greet(readers[1:]))
-    always = z_peers[::-1] + team[::-1] + x_peers
-    greet(always)
-
     amp_copy = pltpu.make_async_copy(amp_hbm, amp_v, copy_sems.at[0])
     amp_copy.start()
     own_copy = pltpu.make_async_copy(owner_hbm.at[rows_at(r * row_tiles, row_tiles)], own_s, copy_sems.at[1])
     own_copy.start()
     w_copy = pltpu.make_async_copy(w_hbm, w_v, copy_sems.at[2])
     w_copy.start()
+
+    barrier = pltpu.get_barrier_semaphore()
+    ahead = zh == 0
+    answering = (zh == 1) & (zl // 4 == 0)
+
+    def greet(peers):
+        for peer in peers:
+            pl.semaphore_signal(barrier, inc=1, device_id=peer, device_id_type=MESH)
+
+    pl.when(jnp.logical_not(answering))(lambda: greet(writers))
+    pl.when(ahead)(lambda: greet(readers[1:]))
+    always = z_peers[::-1] + team[::-1] + x_peers
+    greet(always)
 
     amp_copy.wait()
     mine = rows_at(x * chunk + zl * shard, shard, 32)
@@ -163,7 +163,7 @@
     def share():
         for l in range(2):
             remote(ar.at[mine], ac.at[slot], ci_sems.at[0, 0], ci_sems.at[1, l], writers[l]).wait_recv()
-        for copy in reversed(ga):
+        for copy in (ga[m] for m in (4, 3, 6, 5, 2, 1, 0)):
             copy.start()
 
     outs = [(zl ^ q, 1, (q - 1,)) for q in (7, 6, 5, 4)] + [groups[0]]
@@ -191,7 +191,7 @@
     def col_terms():
         col_all[...] = pack(jnp.dot(wat[...], ar[...], preferred_element_type=F32), occ)
         out = []
-        for m in reversed(range(len(team))):
+        for m in (4, 3, 6, 5, 2, 1, 0):
             yy, cc = mates[m]
             part = rows_at(cc * packed + pair_of(yy) * 2 * piece, 2 * piece)
             out.append(start(col_all.at[part], team_recv.at[m], gd_sems.at[0, m], gd_sems.at[1, m], team[m]))

time: 41.6 us -> 41.6 us (level)
  no operation moved by 1% of the time
where the time goes in v7:
time: 41.6 us; the launch traced here: 41.4 us
  Pallas kernels  40.8 us (98%)
  local copies, waits for them, and re-layouts  0.61 us (1%)
    pallas_call x1, Pallas kernels, local(): pl.pallas_call(kernel, out_shape=pltpu.VMEM((shard, occ), F32), in_specs=...  40.8 us

profile of v7, /device:TPU:1, one launch (start us, length us, event | category | flops | bytes accessed | tf_op | source)
XLA Modules:
  0.0 41.4 jit_solution(2566168859762115928)
XLA Ops:
  0.0 40.8 %shard_map.37 = f32[32,96]{1,0:T(8,128)S(1)} custom-call(bf16[32,96]{1,0:T(8,128)(2,1)} %bitcast.3, bf16[1024,512]{1,0:T(8,128)(2,1)} %w_hbm.1, s32[128,128]{1,0:T(8,128)} %owner_hbm.1), custom_call_target="tpu_custom_call" | custom-call | tf_op jit(solution)/shard_map/pallas_call | solution.py:267
  40.8 0.6 %copy.5 = f32[96,32]{0,1:T(8,128)} copy(f32[96,32]{0,1:T(8,128)S(1)} %bitcast.2) | data formatting | bytes 24576
